TPU v7x, 256 devices: a whole 4x4x8 slice. The times are simulated.
256 devices in a mesh: sub: 32 (over z, x), loc: 8 (over y, core).
Axes of the slice: x: 4, y: 4, z: 8, core: 2. Of those that a mesh axis runs over, the one named last changes fastest.
Arguments:
- partials: float32 [512, 8, 128, 256], P('sub', None, 'loc'), may hold values from -20 to 20
- local_schur: float32 [512, 8, 128, 1024], P('sub', None, 'loc'), may hold values from -1 to 2
- rigid_basis: float32 [512, 6, 8, 128], P('sub', None, None, 'loc'), may hold values from -0.1875 to 0.1875
- coarse_inverse: float32 [1536, 1536], P('sub', 'loc'), may hold values from -1 to 1
- placement: int32 [32], replicated, may hold values from 1 to 13, 160 in all
- neighbour_sub: int32 [256, 8], replicated, may hold values from -1 to 255, as said below
- neighbour_tile: int32 [256, 8], replicated, may hold values from -1 to 7, as said below
- coarse_number: int32 [1536], replicated, may hold values from 0 to 1535, each once
Outputs:
- precond: float32 [512, 8, 128, 256], P('sub', None, 'loc')
- inner_sums: float32 [256], replicated
Inputs may be any that keep to these rules, and one draw needn't show every extreme that they name: Owner o holds placement[o] + 3 subdomains. Where neighbour_sub[s, t] = s2 >= 0: s2 != s, |s2 - s| <= 4, neighbour_sub[s2, neighbour_tile[s, t]] = s and neighbour_tile[s2, neighbour_tile[s, t]] = t; no two tiles of s share one tile of s2. neighbour_tile is -1 exactly where neighbour_sub is. `coarse_number`: each coarse unknown once.
All inputs are finite; a program needn't handle non-finite values.
Results may differ from a plain program's by a relative error of at most 0.000054.
Values sent between devices are 32-bit elements; how exact they have to be, the bound alone decides.
A program may use at most 128 MiB of HBM per device.

v0:
```python
import jax
import jax.numpy as jnp
from jax import lax
from jax.sharding import PartitionSpec as P

SLAB = 4


precise = lax.Precision.HIGHEST


def from_behind(shard, axis, by):
    peers = lax.axis_size(axis)
    pairs = [(i, i + by) for i in range(peers) if 0 <= i + by < peers]
    return lax.ppermute(shard, axis, pairs)


def assemble(values, layout_info):
    partner, their_tile, linked, start_here, count_here, count_left = layout_info
    slot_count = values.shape[0]
    end_here = start_here + count_here
    from_left = from_behind(values, "sub", 1)
    from_right = from_behind(values, "sub", -1)
    left_base = start_here - count_left
    pooled = jnp.concatenate([from_left, values, from_right], axis=0)
    position = jnp.where(
        partner < start_here,
        partner - left_base,
        jnp.where(
            partner < end_here,
            slot_count + partner - start_here,
            slot_count + slot_count + partner - end_here,
        ),
    )
    position = jnp.where(linked, position, 0)
    tile_pick = jnp.where(linked, their_tile, 0)
    mate_values = pooled[position, tile_pick]
    return values + jnp.where(linked[:, :, None, None], mate_values, 0.0)


def local(
    partials,
    local_schur,
    rigid_basis,
    coarse_inverse,
    placement,
    neighbour_sub,
    neighbour_tile,
    coarse_number,
):
    slot_count, tile_count, local_rows, columns = partials.shape
    owner_index = lax.axis_index("sub")
    owner_load = placement + (SLAB - 1)
    starts = jnp.cumsum(owner_load) - owner_load
    count_here = owner_load[owner_index]
    start_here = starts[owner_index]
    count_left = owner_load[jnp.maximum(owner_index - 1, 0)]
    slot_ids = jnp.arange(slot_count, dtype=jnp.int32)
    live_slot = slot_ids < count_here
    last_sub = neighbour_sub.shape[0] - 1
    global_id = jnp.minimum(start_here + slot_ids, last_sub)
    partner = neighbour_sub[global_id]
    linked = (partner >= 0) & live_slot[:, None]
    layout_info = (partner, neighbour_tile[global_id], linked, start_here, count_here, count_left)
    weight = (jnp.where(linked, 0.5, 1.0) * live_slot[:, None]).astype(jnp.float32)[
        :, :, None, None
    ]
    residual = assemble(partials, layout_info)
    scaled = weight * residual
    full_rows = local_schur.shape[3] // tile_count
    schur_view = local_schur.reshape(slot_count, tile_count * local_rows, tile_count, full_rows)
    applied = jnp.einsum(
        "sakc,skcn->san",
        schur_view,
        lax.all_gather(scaled, "loc", axis=2, tiled=True),
        precision=precise,
        preferred_element_type=jnp.float32,
    )
    applied = applied.reshape(slot_count, tile_count, local_rows, columns)
    mode_count = rigid_basis.shape[1]
    coarse_total = coarse_number.shape[0]
    coarse_part = jnp.einsum("smtr,strn->smn", rigid_basis, scaled, precision=precise)
    mode_ids = jnp.arange(mode_count, dtype=jnp.int32)
    coarse_rows = coarse_number[global_id[:, None] * mode_count + mode_ids[None, :]]
    target_rows = jnp.where(live_slot[:, None], coarse_rows, coarse_total)
    block_rows = coarse_inverse.shape[1]
    spread = (
        jnp.zeros((coarse_total, columns), jnp.float32)
        .at[target_rows.reshape(-1)]
        .add(coarse_part.reshape(slot_count * mode_count, columns), mode="drop")
    )
    summed = lax.psum(spread, ("sub", "loc"))
    rhs_block = lax.dynamic_slice_in_dim(summed, lax.axis_index("loc") * block_rows, block_rows, 0)
    partial_solution = jnp.dot(
        coarse_inverse, rhs_block, precision=precise, preferred_element_type=jnp.float32
    )
    solution_rows = lax.psum(partial_solution, "loc")
    all_modes = lax.all_gather(solution_rows, "sub", axis=0, tiled=True)
    mode_values = all_modes[jnp.where(live_slot[:, None], coarse_rows, 0)]
    mode_values = jnp.where(live_slot[:, None, None], mode_values, 0.0)
    corrected = applied + jnp.einsum("smtr,smn->strn", rigid_basis, mode_values, precision=precise)
    weighted = weight * corrected
    assembled = assemble(weighted, layout_info)
    inner_sums = lax.psum(jnp.sum(weight * residual * assembled, axis=(0, 1, 2)), ("sub", "loc"))
    precond = jnp.where(live_slot[:, None, None, None], assembled, 0.0)
    return (precond, inner_sums)


def solution(mesh):
    return jax.shard_map(
        local,
        mesh=mesh,
        in_specs=(
            P("sub", None, "loc", None),
            P("sub", None, "loc", None),
            P("sub", None, None, "loc"),
            P("sub", "loc"),
            P(),
            P(),
            P(),
            P(),
        ),
        out_specs=(P("sub", None, "loc", None), P()),
        check_vma=False,
    )
```

profile of v0, /device:TPU:8, one launch (start us, length us, event | category | flops | bytes accessed | tf_op | source)
XLA Modules:
  0.0 699.6 jit_solution(5522494230847665623)
XLA Ops:
  7.2 0.0 copy-start
  7.2 0.0 all-reduce.2.cloned.1.call-start
  7.2 4.9 collective-permute-start
  12.1 1.3 collective-permute-start.1
  13.4 0.7 fusion.22
  14.1 0.1 copy.20
  14.2 0.1 reduce-window.9
  14.2 0.1 reduce
  14.3 0.7 fusion.21
  15.0 0.6 dynamic_slice.13
  15.6 0.6 fusion.24
  18.7 0.8 copy.21
  19.6 0.7 fusion.17
  20.3 0.6 gather_fusion
  20.8 0.7 select_select_fusion
  21.5 0.1 copy.23
  21.5 0.6 iota_compare_fusion
  22.2 0.1 select_multiply_fusion
  22.3 0.1 copy.22
  22.3 0.8 copy.24
  23.2 0.6 gather_fusion.1
  23.7 0.1 copy.25
  23.8 0.1 copy.26
  23.9 0.1 reshape.385
  24.0 0.7 minimum_multiply_fusion
  24.6 0.1 compare_select_fusion.1
  24.7 0.1 reshape.393
  24.8 0.0 copy-start.5
  24.8 1.1 gather_fusion.3
  26.0 0.1 reshape.392
  26.1 0.1 broadcast_select_fusion.1
  26.2 0.1 select_n.182
  26.3 29.7 %collective-permute-done = f32[16,8,16,256]{3,2,1,0:T(8,128)} collective-permute-done((f32[16,8,16,256]{3,2,1,0:T(8,128)}, f32[16,8,16,256]{3,2,1,0:T(8,128)}, u32[]{:S(2)}, u32[]{:S(2)}) %collective-permute-start) | collective-permute-done | bytes 2097184 | tf_op jit(solution)/shard_map/ppermute | solution.py:15
  56.0 5.5 collective-permute-done.1
  61.4 5.8 pad_maximum_fusion
  67.2 5.0 gather_fusion.2
  72.2 2.6 add_multiply_fusion
  74.8 1.3 convolution_bitcast_fusion
  76.2 2.3 scatter_custom_fusion
  78.5 0.0 all-reduce.2.cloned.1.call-update
  78.5 0.0 all-gather.5.cloned.1.call-start
  78.5 262.7 %all-reduce.2.cloned.1.call-done = f32[1536,256]{1,0:T(8,128)} async-done(((f32[1536,256]{1,0:T(8,128)}), f32[1536,256]{1,0:T(8,128)}) %all-reduce.2.cloned.1.call-update) | async-done | bytes 1572880 | tf_op jit(solution)/shard_map/psum | solution.py:92
  341.3 1.2 convolution_bitcast_fusion.1
  342.5 22.2 %psum.22 = f32[48,256]{1,0:T(8,128)} all-reduce(f32[48,256]{1,0:T(8,128)S(1)} %convolution_bitcast_fusion.1), channel_id=1, replica_groups=mesh['sub'=32,'loc'=8] {'loc'}, use_global_device_ids=true, to_apply=%region_3.4 | all-reduce | flops 12288 | bytes 98304 | tf_op jit(solution)/shard_map/psum | solution.py:97
  364.6 0.0 all-gather.5.cloned.1.call-update
  364.6 0.2 all-gather.3.cloned.1.call-start
  364.9 0.5 all-gather.3.cloned.1.call-update
  365.4 0.1 gather.27
  365.5 8.7 %copy.33 = f32[256,8,8,128]{3,2,1,0:T(8,128)} copy(f32[256,8,8,128]{3,1,2,0:T(8,128)} %bitcast.63) | data formatting | bytes 16777216
  374.1 0.1 compare_select_fusion
  374.2 0.1 reshape.401
  374.3 67.8 %all-gather.5.cloned.1.call-done = f32[1536,256]{1,0:T(8,128)} async-done(((f32[48,256]{1,0:T(8,128)}), f32[1536,256]{1,0:T(8,128)}) %all-gather.5.cloned.1.call-update) | async-done | bytes 1572880 | tf_op jit(solution)/shard_map/all_gather | solution.py:98
  442.1 2.1 gather_fusion.4
  444.2 85.0 %all-gather.3.cloned.1.call-done = f32[16,8,128,256]{3,2,1,0:T(8,128)} async-done(((f32[16,8,16,256]{3,2,1,0:T(8,128)}), f32[16,8,128,256]{3,2,1,0:T(8,128)}) %all-gather.3.cloned.1.call-update) | async-done | bytes 16777232 | tf_op jit(solution)/shard_map/all_gather | solution.py:75
  529.3 16.1 %fusion = f32[16,256,128,1]{1,2,3,0:T(8,128)S(1)} fusion(f32[16,8,128,256]{3,2,1,0:T(8,128)} %all-gather.3.cloned.1.call-done, f32[16,128,8,128]{3,2,1,0:T(8,128)} %bitcast.60), kind=kOutput, calls=%fused_computation.7 | convolution fusion | flops 6442450944 | bytes 27262976 | tf_op jit(solution)/shard_map/sakc,skcn->san/dot_general | solution.py:72
  545.4 2.4 fusion.2
  547.8 3.5 collective-permute-start.2
  551.3 1.5 collective-permute-start.3
  552.9 43.6 %collective-permute-done.2 = f32[16,8,16,256]{3,2,1,0:T(8,128)S(1)} collective-permute-done((f32[16,8,16,256]{3,2,1,0:T(8,128)S(1)}, f32[16,8,16,256]{3,2,1,0:T(8,128)S(1)}, u32[]{:S(2)}, u32[]{:S(2)}) %collective-permute-start.2) | collective-permute-done | bytes 2097184 | tf_op jit(solution)/shard_map/ppermute | solution.py:15
  596.5 4.2 collective-permute-done.3
  600.8 3.4 pad_maximum_fusion.1
  604.2 5.1 gather_fusion.5
  609.3 4.9 multiply_reduce_fusion
  614.3 78.8 %psum.23 = f32[256]{0:T(256)} all-reduce(f32[256]{0:T(256)S(1)} %get-tuple-element.5), channel_id=1, replica_groups=mesh['sub'=32,'loc'=8] {'sub','loc'}, use_global_device_ids=true, to_apply=%region_5.6 | all-reduce | flops 256 | bytes 2048 | tf_op jit(solution)/shard_map/psum | solution.py:104
  (19 shorter events, 0.1 us)
Async XLA Ops:
  7.2 67.6 %copy-start = (f32[16,6,8,16]{3,2,1,0:T(8,128)S(1)}, f32[16,6,8,16]{3,2,1,0:T(8,128)}, u32[]{:S(2)}) copy-start(f32[16,6,8,16]{3,2,1,0:T(8,128)} %param.10) | copy-start | bytes 147460
  7.2 17.6 %copy-start.1 = (s32[1536]{0:T(1024)S(1)}, s32[1536]{0:T(1024)}, u32[]{:S(2)}) copy-start(s32[1536]{0:T(1024)} %param.15) | copy-start | bytes 18436
  7.2 334.1 %all-reduce.2.cloned.1.call-start = ((), (), s32[]{:S(2)}) async-start(), calls=%async_computation.1 | async-start | bytes 3145728 | tf_op jit(solution)/shard_map/psum | solution.py:92
  7.2 48.7 %collective-permute-start = (f32[16,8,16,256]{3,2,1,0:T(8,128)}, f32[16,8,16,256]{3,2,1,0:T(8,128)}, u32[]{:S(2)}, u32[]{:S(2)}) collective-permute-start(f32[16,8,16,256]{3,2,1,0:T(8,128)} %param.8), channel_id=1, source_target_pairs={{0,8},{8,16},{16,24},{24,32},{32,40},{40,48},{48,56},{56,64},{64,7... | collective-permute-start | bytes 6291464 | tf_op jit(solution)/shard_map/ppermute | solution.py:15
  12.1 49.3 %collective-permute-start.1 = (f32[16,8,16,256]{3,2,1,0:T(8,128)}, f32[16,8,16,256]{3,2,1,0:T(8,128)}, u32[]{:S(2)}, u32[]{:S(2)}) collective-permute-start(f32[16,8,16,256]{3,2,1,0:T(8,128)} %param.8), channel_id=1, source_target_pairs={{8,0},{16,8},{24,16},{32,24},{40,32},{48,40},{56,48},{64,56},{72,6... | collective-permute-start | bytes 6291464 | tf_op jit(solution)/shard_map/ppermute | solution.py:15
  24.8 36.6 %copy-start.5 = (f32[16,8,16,256]{3,2,1,0:T(8,128)S(1)}, f32[16,8,16,256]{3,2,1,0:T(8,128)}, u32[]{:S(2)}) copy-start(f32[16,8,16,256]{3,2,1,0:T(8,128)} %param.8) | copy-start | bytes 6291460
  74.8 3.7 copy-start.2
  76.1 265.2 %copy-start.6 = (f32[48,192]{1,0:T(8,128)S(1)}, f32[48,192]{1,0:T(8,128)}, u32[]{:S(2)}) copy-start(f32[48,192]{1,0:T(8,128)} %param.11) | copy-start | bytes 110596
  78.5 363.6 %all-gather.5.cloned.1.call-start = ((), (), s32[]{:S(2)}) async-start(), calls=%async_computation.2 | async-start | bytes 1622016 | tf_op jit(solution)/shard_map/all_gather | solution.py:98
  364.6 164.6 %all-gather.3.cloned.1.call-start = ((), (), s32[]{:S(2)}) async-start(), calls=%async_computation | async-start | bytes 18874368 | tf_op jit(solution)/shard_map/all_gather | solution.py:75
  547.8 52.9 %copy-start.4 = (f32[16,8,16,256]{3,2,1,0:T(8,128)}, f32[16,8,16,256]{3,2,1,0:T(8,128)S(1)}, u32[]{:S(2)}) copy-start(f32[16,8,16,256]{3,2,1,0:T(8,128)S(1)} %fusion.2) | copy-start | bytes 6291460
  547.8 48.7 %collective-permute-start.2 = (f32[16,8,16,256]{3,2,1,0:T(8,128)S(1)}, f32[16,8,16,256]{3,2,1,0:T(8,128)S(1)}, u32[]{:S(2)}, u32[]{:S(2)}) collective-permute-start(f32[16,8,16,256]{3,2,1,0:T(8,128)S(1)} %fusion.2), channel_id=1, source_target_pairs={{0,8},{8,16},{16,24},{24,32},{32,40},{40,48},{48,56},{56,64},{64,7... | collective-permute-start | bytes 6291464 | tf_op jit(solution)/shard_map/ppermute | solution.py:15
  551.3 49.4 %collective-permute-start.3 = (f32[16,8,16,256]{3,2,1,0:T(8,128)S(1)}, f32[16,8,16,256]{3,2,1,0:T(8,128)S(1)}, u32[]{:S(2)}, u32[]{:S(2)}) collective-permute-start(f32[16,8,16,256]{3,2,1,0:T(8,128)S(1)} %fusion.2), channel_id=1, source_target_pairs={{8,0},{16,8},{24,16},{32,24},{40,32},{48,40},{56,48},{64,56},{72,6... | collective-permute-start | bytes 6291464 | tf_op jit(solution)/shard_map/ppermute | solution.py:15
  604.2 5.1 copy-start.3
Sparse Core Ops, SparseCore 0:
  78.6 262.6 all-reduce.1
  364.8 77.3 all-gather.4
  444.7 84.5 all-gather.2
where the time goes:
time: 702 us; the launch traced here: 700 us
  waiting for transfers between devices  499 us (71%)
  blocking collectives  101 us (14%)
  local copies, waits for them, and re-layouts  27 us (4%)
  other arithmetic  23.4 us (3%)
  matrix products  21 us (3%)
  between operations  16.6 us (2%)
  starting transfers between devices  11.5 us (2%)
    psum x1, waiting for transfers between devices, local(): summed = lax.psum(spread, ('sub', 'loc'))  263 us
    all_gather x1, waiting for transfers between devices, local(): lax.all_gather(scaled, 'loc', axis=2, tiled=True)  85 us
    ppermute x4, waiting for transfers between devices, from_behind(): return lax.ppermute(shard, axis, pairs)  83 us
    psum x1, blocking collectives, local(): lax.psum(jnp.sum(weight * residual * assembled, axis=(0, 1, 2)), ('sub',...  78.8 us
    all_gather x1, waiting for transfers between devices, local(): all_modes = lax.all_gather(solution_rows, 'sub', axis=0, tiled=True)  67.8 us
    psum x1, blocking collectives, local(): solution_rows = lax.psum(partial_solution, 'loc')  22.2 us
    dot_general x1, matrix products, local(): jnp.einsum('sakc,skcn->san', schur_view, lax.all_gather(scaled, 'loc', ax...  16.1 us
  transfers between devices with their start and end apart: 7, of which 7 were waited for; matrix products, arithmetic and copies ran while one was open for 3% of the time, Pallas kernels for 0%

commit v1 on v0

v1 whole, which is shorter than its diff:
```python
import functools
import jax
import jax.numpy as jnp
from jax import lax
from jax.experimental import pallas as pl
from jax.experimental.pallas import tpu as pltpu
from jax.sharding import PartitionSpec as P

SLAB = 4
X = 4
MESH = pl.DeviceIdType.MESH
HI = lax.Precision.HIGHEST
F32 = jnp.float32


def dot(a, b, dims=(((1,), (0,)), ((), ()))):
    return lax.dot_general(a, b, dims, precision=HI, preferred_element_type=F32)


def kernel(
    n_sub,
    n_loc,
    part_hbm,
    schur_hbm,
    basis,
    inv,
    placement,
    nsub,
    ntile,
    cnum,
    out,
    inner_out,
    PV,
    SV,
    SC,
    G,
    V,
    H1,
    H2,
    SB1,
    SB2,
    CP,
    CT,
    R1,
    R2,
    R3,
    M4,
    MV,
    IF,
    IT,
    W,
    IS1,
    IS2,
    IS3,
    ACC,
    ld,
    hs,
    hr,
    cs,
    cr,
    ysend,
    ra,
    rb,
    ha,
    hb,
    rs,
):
    Z = n_sub // X
    Y = n_loc // 2
    slots, tiles, rl, cols = PV.shape
    subs = nsub.shape[1]
    rows_here = tiles * rl
    modes = 6
    pad = 8
    nb = cols // n_loc
    io, ic = inv.shape

    o = lax.axis_index("sub")
    l = lax.axis_index("loc")
    z, x = o // X, o % X
    y, c = l // 2, l % 2
    lp = 2 * ((y + 1) % Y) + c
    lm = 2 * ((y + Y - 1) % Y) + c
    l2 = 2 * ((y + 2) % Y) + c
    sib = 2 * y + (1 - c)
    right, left = (o + 1) % n_sub, (o + n_sub - 1) % n_sub

    def rcopy(src, dst, send, recv, dev):
        return pltpu.make_async_remote_copy(
            src_ref=src, dst_ref=dst, send_sem=send, recv_sem=recv, device_id=dev, device_id_type=MESH
        )

    def wait_recv(ref, sem):
        rcopy(ref, ref, sem, sem, (o, sib)).wait_recv()

    def wait_send(ref, sem):
        rcopy(ref, ref, sem, sem, (o, sib)).wait_send()

    load_p = pltpu.make_async_copy(part_hbm, PV, ld.at[0])
    load_s = pltpu.make_async_copy(schur_hbm, SV, ld.at[1])
    load_p.start()
    load_s.start()

    barrier = pltpu.get_barrier_semaphore()
    peers = [(right, l), (left, l)]
    peers += [(o, (l + i) % n_loc) for i in range(1, n_loc)]
    peers += [(z * X + (x + i) % X, l) for i in range(1, X)]
    peers += [(((z + i) % Z) * X + x, l) for i in range(1, Z)]
    for peer in peers:
        pl.semaphore_signal(barrier, inc=1, device_id=peer, device_id_type=MESH)

    def load_of(i):
        return placement[i] + (SLAB - 1)

    start = lax.fori_loop(
        0, n_sub, lambda i, acc: acc + jnp.where(i < o, load_of(i), 0), jnp.int32(0)
    )
    cnt = load_of(o)

    def slot_of(p):
        group, i = p // 4, p % 4
        inner = jnp.where(group == 0, 4, 8) + i
        j_right = cnt - 4 + i
        slot = jnp.where(group == 1, j_right, jnp.where(group == 2, i, inner))
        live = jnp.where(group == 1, j_right >= 4, (group == 2) | (inner < cnt - 4))
        return jnp.clip(slot, 0, slots - 1), live

    def pos_of(j):
        p = jnp.where(
            j < 4,
            8 + j,
            jnp.where(j >= cnt - 4, 4 + j - (cnt - 4), jnp.where(j < 8, j - 4, j + 4)),
        )
        return jnp.clip(p, 0, slots - 1)

    def link(j, live, t):
        sid = jnp.clip(start + j, 0, subs - 1)
        partner = nsub[t, sid]
        mate = jnp.clip(ntile[t, sid], 0, tiles - 1)
        linked = (partner >= 0) & live
        q = partner - start
        own = (q >= 0) & (q < cnt)
        hq = jnp.clip(jnp.where(q < 0, 4 + q, 4 + q - cnt), 0, 7)
        return linked, own, jnp.clip(q, 0, slots - 1), hq, mate

    def residual(p, halo):
        j, live = slot_of(p)
        for t in range(tiles):
            linked, own, q, hq, mt = link(j, live, t)
            other = PV[q, mt]
            if halo:
                other = jnp.where(own, other, H1[hq, mt])
            res = PV[j, t] + jnp.where(linked, other, 0.0)
            w = jnp.where(linked, 0.5, 1.0)
            val = jnp.where(live, w * res, 0.0)
            SC[p, t] = val
            G[p, t, l] = val

    def send_own(p):
        src = SC.at[p]
        dst = G.at[p, :, l]
        rcopy(src, dst, ysend, ra.at[p], (o, lp)).start()
        rcopy(src, dst, ysend, rb.at[p], (o, lm)).start()
        rcopy(src, dst, ysend, rs.at[p], (o, sib)).start()

    def forward(p):
        wait_recv(G.at[p, :, lm], ra.at[p])
        half = G.at[p, : tiles // 2, lm]
        rcopy(half, half, ysend, ha.at[p], (o, lp)).start()
        whole = G.at[p, :, lm]
        rcopy(whole, whole, ysend, rs.at[p], (o, sib)).start()
        wait_recv(G.at[p, :, lp], rb.at[p])
        half = G.at[p, tiles // 2 :, lp]
        rcopy(half, half, ysend, hb.at[p], (o, lm)).start()
        whole = G.at[p, :, lp]
        rcopy(whole, whole, ysend, rs.at[p], (o, sib)).start()

    def halves(p):
        wait_recv(G.at[p, : tiles // 2, l2], ha.at[p])
        wait_recv(G.at[p, tiles // 2 :, l2], hb.at[p])
        whole = G.at[p, :, l2]
        rcopy(whole, whole, ysend, rs.at[p], (o, sib)).start()

    def apply_local(p):
        wait_recv(G.at[p, :, : n_loc // 2], rs.at[p])
        j, _ = slot_of(p)
        a = SV[j].reshape(rows_here, tiles * n_loc * rl)
        b = G[p].reshape(tiles * n_loc * rl, cols)
        V[p] = dot(a, b).reshape(tiles, rl, cols)

    def correct(p):
        j, live = slot_of(p)
        corr = dot(basis[j], MV[j], (((0,), (0,)), ((), ())))
        val = V[p] + corr.reshape(tiles, rl, cols)
        acc = ACC[...]
        for t in range(tiles):
            linked, _, _, _, _ = link(j, live, t)
            w = jnp.where(linked, 0.5, 1.0)
            acc = acc + SC[p, t] * val[t]
            V[p, t] = jnp.where(live, w * val[t], 0.0)
        ACC[...] = acc

    def loc_spread(src_of, buf, k):
        for i in range(1, n_loc):
            peer = (l + i) % n_loc
            rcopy(src_of(peer), buf.at[l], cs.at[k], cr.at[k], (o, peer)).start()

    def loc_wait(buf, k):
        wait_recv(buf.at[: n_loc - 1], cr.at[k])

    def x_spread(buf, k):
        for i in range(1, X):
            peer = z * X + (x + i) % X
            rcopy(buf.at[o], buf.at[o], cs.at[k], cr.at[k], (peer, l)).start()

    def x_wait(buf, k):
        wait_recv(buf.at[: X - 1], cr.at[k])

    def z_spread(buf, k):
        block = buf.at[pl.ds(z * X, X)]
        for i in range(1, Z):
            peer = ((z + i) % Z) * X + x
            rcopy(block, block, cs.at[k], cr.at[k], (peer, l)).start()

    def z_wait(buf, k):
        wait_recv(buf.at[: (Z - 1) * X], cr.at[k])

    load_p.wait()

    for i in range(4):
        for t in range(tiles):
            SB1[i, t] = PV[jnp.clip(cnt - 4 + i, 0, slots - 1), t]

    pl.semaphore_wait(barrier, len(peers))

    to_left = rcopy(PV.at[:4], H1.at[4:], hs.at[0], hr.at[0], (left, l))
    to_right = rcopy(SB1, H1.at[:4], hs.at[1], hr.at[1], (right, l))
    to_left.start()
    to_right.start()
    IF[l] = inv[...]
    loc_spread(lambda peer: inv, IF, 0)

    def first(p, carry):
        residual(p, False)
        send_own(p)
        return carry

    lax.fori_loop(0, 4, first, 0)

    def second(p, carry):
        residual(p, False)
        return carry

    lax.fori_loop(12, 16, second, 0)

    ACC[...] = jnp.zeros_like(ACC)
    IT[...] = jnp.zeros_like(IT)
    W[...] = jnp.zeros_like(W)
    loc_wait(IF, 0)
    for k in range(n_loc):
        IT[k * ic : (k + 1) * ic, :io] = IF[k].T

    def fill(s, carry):
        for m in range(modes):
            row = jnp.clip(cnum[s * modes + m], 0, n_loc * ic - 1)
            W[s, m : m + 1, :] = IT[pl.ds(row, 1), :]
        return carry

    lax.fori_loop(0, subs, fill, 0)

    to_left.wait_recv()
    to_right.wait_recv()

    def third(p, carry):
        residual(p, True)
        send_own(p)
        return carry

    lax.fori_loop(4, 12, third, 0)

    def fourth(p, carry):
        send_own(p)
        return carry

    lax.fori_loop(12, 16, fourth, 0)

    def coarse_part(j, carry):
        vals = SC[pos_of(j)].reshape(rows_here, cols)
        vals = jnp.where(j < cnt, vals, 0.0)
        CP[j] = dot(basis[j], vals)
        return carry

    lax.fori_loop(0, slots, coarse_part, 0)
    CT[...] = CP[...].reshape(slots * pad, cols).T.reshape(n_loc, nb, slots * pad)
    R1[l] = CT[l]
    loc_spread(lambda peer: CT.at[peer], R1, 1)

    def reduce_loc():
        loc_wait(R1, 1)
        total = R1[0]
        for i in range(1, n_loc):
            total = total + R1[i]
        R2[o] = total
        x_spread(R2, 2)

    def gather_z():
        x_wait(R2, 2)
        z_spread(R2, 3)

    def solve():
        z_wait(R2, 3)

        def body(k, carry):
            total, at = carry
            rows = W[pl.ds(jnp.clip(at, 0, subs), slots)].reshape(slots * pad, 128)
            total = total + dot(R2[k], rows)
            return total, at + load_of(k)

        total, _ = lax.fori_loop(0, n_sub, body, (jnp.zeros((nb, 128), F32), jnp.int32(0)))
        R3[o] = total
        x_spread(R3, 4)

    def gather_z2():
        x_wait(R3, 4)
        z_spread(R3, 5)

    def select():
        z_wait(R3, 5)
        lanes = lax.broadcasted_iota(jnp.int32, (8, 128), 1)

        def number(j, v):
            sid = jnp.clip(start + j, 0, subs - 1)
            for m in range(modes):
                row = cnum[sid * modes + m]
                v = jnp.where((lanes == j * pad + m) & (j < cnt), row, v)
            return v

        numbers = lax.fori_loop(0, slots, number, jnp.full((8, 128), -1, jnp.int32))
        wanted = jnp.broadcast_to(numbers[:1], (128, 128))
        rows = lax.broadcasted_iota(jnp.int32, (128, 128), 0)

        def body(k, total):
            hot = ((wanted == rows + k * io) & (rows < io)).astype(F32).astype(jnp.bfloat16)
            v = R3[k]
            h = v.astype(jnp.bfloat16)
            r = v - h.astype(F32)
            m = r.astype(jnp.bfloat16)
            q = (r - m.astype(F32)).astype(jnp.bfloat16)
            for part in (h, m, q):
                total = total + lax.dot_general(
                    part, hot, (((1,), (0,)), ((), ())), preferred_element_type=F32
                )
            return total

        mv = lax.fori_loop(0, n_sub, body, jnp.zeros((nb, 128), F32))
        M4[l] = mv
        loc_spread(lambda peer: M4.at[l], M4, 6)

    MV_AT = 10

    def modes_ready():
        loc_wait(M4, 6)
        MV[...] = M4[...].reshape(cols, 128).T.reshape(slots, pad, cols)

        def body(p, carry):
            correct(p)
            return carry

        lax.fori_loop(0, MV_AT - 1, body, 0)

    def send_halo():
        for i in range(4):
            p = pos_of(cnt - 4 + i)
            for t in range(tiles):
                SB2[i, t] = V[p, t]
        rcopy(V.at[8:12], H2.at[4:], hs.at[2], hr.at[2], (left, l)).start()
        rcopy(SB2, H2.at[:4], hs.at[3], hr.at[3], (right, l)).start()

    chain = {2: reduce_loc, 3: gather_z, 4: solve, 5: gather_z2, 6: select, MV_AT: modes_ready, 13: send_halo}

    load_s.wait()

    def step(s, carry):
        @pl.when(s < slots)
        def _():
            forward(s)

        @pl.when((s >= 1) & (s < slots + 1))
        def _():
            halves(s - 1)

        @pl.when(s >= 2)
        def _():
            apply_local(s - 2)

        @pl.when(s > MV_AT)
        def _():
            correct(s - 2)

        for at, what in chain.items():
            pl.when(s == at)(what)
        return carry

    lax.fori_loop(0, slots + 2, step, 0)

    IS1[l] = ACC[: rl // 2, :] + ACC[rl // 2 :, :]
    loc_spread(lambda peer: IS1.at[l], IS1, 7)

    wait_recv(H2.at[4:], hr.at[2])
    wait_recv(H2.at[:4], hr.at[3])

    def finish(j, carry):
        live = j < cnt
        p = pos_of(j)
        for t in range(tiles):
            linked, own, q, hq, mt = link(j, live, t)
            other = jnp.where(own, V[pos_of(q), mt], H2[hq, mt])
            val = V[p, t] + jnp.where(linked, other, 0.0)
            out[j, t] = jnp.where(live, val, 0.0)
        return carry

    lax.fori_loop(0, 6, finish, 0)
    loc_wait(IS1, 7)
    total = IS1[0]
    for i in range(1, n_loc):
        total = total + IS1[i]
    IS2[x] = total
    for i in range(1, X):
        peer = z * X + (x + i) % X
        rcopy(IS2.at[x], IS2.at[x], cs.at[8], cr.at[8], (peer, l)).start()
    lax.fori_loop(6, 11, finish, 0)
    wait_recv(IS2.at[: X - 1], cr.at[8])
    total = IS2[0]
    for i in range(1, X):
        total = total + IS2[i]
    IS3[z] = total
    for i in range(1, Z):
        peer = ((z + i) % Z) * X + x
        rcopy(IS3.at[z], IS3.at[z], cs.at[9], cr.at[9], (peer, l)).start()
    lax.fori_loop(11, 16, finish, 0)
    wait_recv(IS3.at[: Z - 1], cr.at[9])
    total = IS3[0]
    for i in range(1, Z):
        total = total + IS3[i]
    inner_out[...] = jnp.sum(total, axis=0, keepdims=True)

    wait_send(PV.at[:4], hs.at[0])
    wait_send(SB1, hs.at[1])
    wait_send(V.at[8:12], hs.at[2])
    wait_send(SB2, hs.at[3])
    wait_send(G.at[:, :, : n_loc - 1], ysend)
    wait_send(IF.at[: n_loc - 1], cs.at[0])
    wait_send(R1.at[: n_loc - 1], cs.at[1])
    wait_send(R2.at[: X - 1], cs.at[2])
    wait_send(R2.at[: (Z - 1) * X], cs.at[3])
    wait_send(R3.at[: X - 1], cs.at[4])
    wait_send(R3.at[: (Z - 1) * X], cs.at[5])
    wait_send(M4.at[: n_loc - 1], cs.at[6])
    wait_send(IS1.at[: n_loc - 1], cs.at[7])
    wait_send(IS2.at[: X - 1], cs.at[8])
    wait_send(IS3.at[: Z - 1], cs.at[9])


def local(n_sub, n_loc, partials, local_schur, rigid_basis, coarse_inverse, placement, nsub, ntile, cnum):
    slots, tiles, rl, cols = partials.shape
    modes = rigid_basis.shape[1]
    subs = nsub.shape[0]
    io, ic = coarse_inverse.shape
    nb = cols // n_loc
    Z = n_sub // X
    basis = jnp.pad(rigid_basis, ((0, 0), (0, 8 - modes), (0, 0), (0, 0))).reshape(slots, 8, tiles * rl)
    vmem = lambda *shape: pltpu.VMEM(shape, F32)
    dma = lambda *shape: pltpu.SemaphoreType.DMA(shape)
    in_v = pl.BlockSpec(memory_space=pltpu.VMEM)
    in_s = pl.BlockSpec(memory_space=pltpu.SMEM)
    any_ = pl.BlockSpec(memory_space=pl.ANY)
    precond, inner = pl.pallas_call(
        functools.partial(kernel, n_sub, n_loc),
        out_shape=(
            jax.ShapeDtypeStruct(partials.shape, F32),
            jax.ShapeDtypeStruct((1, cols), F32),
        ),
        in_specs=[any_, any_, in_v, in_v, in_s, in_s, in_s, in_s],
        out_specs=(in_v, in_v),
        scratch_shapes=[
            vmem(slots, tiles, rl, cols),
            vmem(slots, tiles, rl, tiles * n_loc * rl),
            vmem(slots, tiles, rl, cols),
            vmem(slots, tiles, n_loc, rl, cols),
            vmem(slots, tiles, rl, cols),
            vmem(8, tiles, rl, cols),
            vmem(8, tiles, rl, cols),
            vmem(4, tiles, rl, cols),
            vmem(4, tiles, rl, cols),
            vmem(slots, 8, cols),
            vmem(n_loc, nb, slots * 8),
            vmem(n_loc, nb, slots * 8),
            vmem(n_sub, nb, slots * 8),
            vmem(n_sub, nb, 128),
            vmem(n_loc, nb, 128),
            vmem(slots, 8, cols),
            vmem(n_loc, io, ic),
            vmem(n_loc * ic, 128),
            vmem(subs + slots, 8, 128),
            vmem(n_loc, rl // 2, cols),
            vmem(X, rl // 2, cols),
            vmem(Z, rl // 2, cols),
            vmem(rl, cols),
            dma(2),
            dma(4),
            dma(4),
            dma(10),
            dma(10),
            pltpu.SemaphoreType.DMA,
            dma(slots),
            dma(slots),
            dma(slots),
            dma(slots),
            dma(slots),
        ],
        compiler_params=pltpu.CompilerParams(
            collective_id=0, has_side_effects=True, vmem_limit_bytes=56 * 1024 * 1024
        ),
    )(partials, local_schur, basis, coarse_inverse, placement, nsub.T, ntile.T, cnum)
    return precond, inner.reshape(cols)


def solution(mesh):
    n_sub, n_loc = mesh.shape["sub"], mesh.shape["loc"]
    return jax.shard_map(
        functools.partial(local, n_sub, n_loc),
        mesh=mesh,
        in_specs=(
            P("sub", None, "loc", None),
            P("sub", None, "loc", None),
            P("sub", None, None, "loc"),
            P("sub", "loc"),
            P(),
            P(),
            P(),
            P(),
        ),
        out_specs=(P("sub", None, "loc", None), P()),
        check_vma=False,
    )
```

time: 702 us -> 162 us (0.23)
  waiting for transfers between devices: 499 us -> 0 us
  Pallas kernels: 0 us -> 156 us
  blocking collectives: 101 us -> 0 us
  other arithmetic: 23.4 us -> 0 us
  local copies, waits for them, and re-layouts: 27 us -> 5.58 us
  matrix products: 21 us -> 0 us
  between operations: 16.6 us -> 0.65 us
  starting transfers between devices: 11.5 us -> 0 us
    psum x1 -> x0, waiting for transfers between devices: 263 us -> none  [local(): summed = lax.psum(spread, ('sub', 'loc'))]
    pallas_call x0 -> x1, Pallas kernels: none -> 156 us  [local(): pl.pallas_call(functools.partial(kernel, n_sub, n_loc), out_shape=(jax.Sh...]
    all_gather x2 -> x0, waiting for transfers between devices: 153 us -> none  [the longest x1 85 us: local(): lax.all_gather(scaled, 'loc', axis=2, tiled=True)]
    psum x2 -> x0, blocking collectives: 101 us -> none  [the longest x1 78.8 us: local(): lax.psum(jnp.sum(weight * residual * assembled, axis=(0, 1, 2)), ('sub',...]
    ppermute x4 -> x0, waiting for transfers between devices: 83 us -> none  [from_behind(): return lax.ppermute(shard, axis, pairs)]
    dot_general x4 -> x0, matrix products: 21 us -> none  [the longest x1 16.1 us: local(): jnp.einsum('sakc,skcn->san', schur_view, lax.all_gather(scaled, 'loc', ax...]
    gather x10 -> x0, local copies, waits for them, and re-layouts: 14.7 us -> none  [the longest x2 10.1 us: assemble(): mate_values = pooled[position, tile_pick]]
    ppermute x4 -> x0, starting transfers between devices: 11.2 us -> none  [from_behind(): return lax.ppermute(shard, axis, pairs)]
  transfers between devices with their start and end apart: 7 -> 0, of which waited for: 7 -> 0; matrix products, arithmetic and copies ran while one was open for 3% -> 0% of each run, Pallas kernels for 0% -> 0%
where the time goes in v1:
time: 162 us
  Pallas kernels  156 us (96%)
  local copies, waits for them, and re-layouts  5.58 us (3%)
    pallas_call x1, Pallas kernels, local(): pl.pallas_call(functools.partial(kernel, n_sub, n_loc), out_shape=(jax.Sh...  156 us
    unnamed x4, local copies, waits for them, and re-layouts  3.71 us

profile of v1, /device:TPU:8, one launch (start us, length us, event | category | flops | bytes accessed | tf_op | source)
XLA Modules:
  0.0 161.9 jit_solution(13297668378216513148)
XLA Ops:
  0.6 1.0 pad.4
  1.7 0.8 reshape.10.basis
  2.5 155.7 %shard_map.95 = (f32[16,8,16,256]{3,2,1,0:T(8,128)}, f32[1,256]{1,0:T(1,128)}) custom-call(f32[16,8,16,256]{3,2,1,0:T(8,128)} %part_hbm.1, f32[16,8,16,1024]{3,2,1,0:T(8,128)} %schur_hbm.1, f32[16,8,128]{2,1,0:T(8,128)} %reshape.10.basis, f32[48,192]{1,0:T(8,128)} %inv.1, s32[32]{0:T(128)} %placement.1, s32[8,256]{1,0:T(8,128)} %bitcast.5, ...), custom_call_target="tpu_custom_call" | custom-call | tf_op jit(solution)/shard_map/pallas_call | solution.py:477
  158.2 0.0 copy-start
  158.2 3.1 %copy.12 = f32[16,8,16,256]{3,2,1,0:T(8,128)} copy(f32[16,8,16,256]{3,2,1,0:T(8,128)} %get-tuple-element.8) | data formatting | bytes 4194304
  161.3 0.0 copy-done
  161.3 0.6 copy.13
Async XLA Ops:
  158.2 3.2 %copy-start = (f32[1,256]{1,0:T(1,128)S(1)}, f32[1,256]{1,0:T(1,128)}, u32[]{:S(2)}) copy-start(f32[1,256]{1,0:T(1,128)} %get-tuple-element.5) | copy-start | bytes 3076

commit v2 on v1

--- a/solution.py
+++ b/solution.py
@@ -7,14 +7,39 @@
 from jax.sharding import PartitionSpec as P
 
 SLAB = 4
+EARLY = 6
+LAG = 4
+MV_AT = 12
 X = 4
 MESH = pl.DeviceIdType.MESH
 HI = lax.Precision.HIGHEST
 F32 = jnp.float32
+BF16 = jnp.bfloat16
 
 
 def dot(a, b, dims=(((1,), (0,)), ((), ()))):
     return lax.dot_general(a, b, dims, precision=HI, preferred_element_type=F32)
+
+
+def split3(v):
+    h = v.astype(BF16)
+    r = v - h.astype(F32)
+    m = r.astype(BF16)
+    return h, m, (r - m.astype(F32)).astype(BF16)
+
+
+def mul16(a, b):
+    return lax.dot_general(a, b, (((1,), (0,)), ((), ())), preferred_element_type=F32)
+
+
+def stacked_dot(a, b):
+    n = a.shape[0]
+    ah, am, al = split3(a)
+    bh, bm, bl = split3(b)
+    one = mul16(jnp.concatenate([ah, am, al], axis=0), bh)
+    two = mul16(jnp.concatenate([ah, am], axis=0), bm)
+    low = one[2 * n :] + two[n:] + mul16(ah, bl)
+    return one[:n] + (one[n : 2 * n] + two[:n] + low)
 
 
 def kernel(
@@ -22,14 +47,22 @@
     n_loc,
     part_hbm,
     schur_hbm,
-    basis,
+    basis_hbm,
+    inv_hbm,
+    placement_hbm,
+    nsub_hbm,
+    ntile_hbm,
+    cnum_hbm,
+    out,
+    inner_out,
+    basis_in,
     inv,
     placement,
     nsub,
     ntile,
     cnum,
-    out,
-    inner_out,
+    basis,
+    OUT,
     PV,
     SV,
     SC,
@@ -39,6 +72,7 @@
     H2,
     SB1,
     SB2,
+    CPP,
     CP,
     CT,
     R1,
@@ -54,6 +88,9 @@
     IS3,
     ACC,
     ld,
+    relay,
+    od,
+    ir,
     hs,
     hr,
     cs,
@@ -96,40 +133,52 @@
     def wait_send(ref, sem):
         rcopy(ref, ref, sem, sem, (o, sib)).wait_send()
 
-    load_p = pltpu.make_async_copy(part_hbm, PV, ld.at[0])
-    load_s = pltpu.make_async_copy(schur_hbm, SV, ld.at[1])
-    load_p.start()
-    load_s.start()
+    pairs = [(placement_hbm, placement), (nsub_hbm, nsub), (ntile_hbm, ntile), (part_hbm, PV)]
+    pairs += [(inv_hbm, inv), (basis_hbm, basis_in), (cnum_hbm, cnum), (schur_hbm, SV)]
+    loads = [pltpu.make_async_copy(src, dst, ld.at[k]) for k, (src, dst) in enumerate(pairs)]
+    for load in loads:
+        load.start()
 
     barrier = pltpu.get_barrier_semaphore()
-    peers = [(right, l), (left, l)]
-    peers += [(o, (l + i) % n_loc) for i in range(1, n_loc)]
-    peers += [(z * X + (x + i) % X, l) for i in range(1, X)]
-    peers += [(((z + i) % Z) * X + x, l) for i in range(1, Z)]
+    near = [(o, lp), (o, lm), (o, sib)]
+    near += [(z * X + (x + i) % X, l) for i in (1, X - 1)]
+    near += [(((z + i) % Z) * X + x, l) for i in (1, Z - 1)]
+    peers = near + [(right, l), (left, l)]
     for peer in peers:
         pl.semaphore_signal(barrier, inc=1, device_id=peer, device_id_type=MESH)
 
+    circles = [near, [near[2]] + near[5:], near[5:]]
+
+    def tell(k):
+        for peer in circles[k]:
+            pl.semaphore_signal(relay.at[k], inc=1, device_id=peer, device_id_type=MESH)
+
+    def heard(k):
+        pl.semaphore_wait(relay.at[k], len(circles[k]))
+
     def load_of(i):
         return placement[i] + (SLAB - 1)
 
+    for load in loads[:3]:
+        load.wait()
     start = lax.fori_loop(
         0, n_sub, lambda i, acc: acc + jnp.where(i < o, load_of(i), 0), jnp.int32(0)
     )
     cnt = load_of(o)
 
     def slot_of(p):
-        group, i = p // 4, p % 4
-        inner = jnp.where(group == 0, 4, 8) + i
-        j_right = cnt - 4 + i
-        slot = jnp.where(group == 1, j_right, jnp.where(group == 2, i, inner))
-        live = jnp.where(group == 1, j_right >= 4, (group == 2) | (inner < cnt - 4))
+        inner = jnp.where(p < 4, 4 + p, p - 4)
+        at_left, at_right = (p >= 4) & (p < 8), (p >= 8) & (p < 12)
+        j_right = cnt - 12 + p
+        slot = jnp.where(at_right, j_right, jnp.where(at_left, p - 4, inner))
+        live = jnp.where(at_right, j_right >= 4, at_left | (inner < cnt - 4))
         return jnp.clip(slot, 0, slots - 1), live
 
     def pos_of(j):
         p = jnp.where(
             j < 4,
-            8 + j,
-            jnp.where(j >= cnt - 4, 4 + j - (cnt - 4), jnp.where(j < 8, j - 4, j + 4)),
+            4 + j,
+            jnp.where(j >= cnt - 4, 8 + j - (cnt - 4), jnp.where(j < 8, j - 4, j + 4)),
         )
         return jnp.clip(p, 0, slots - 1)
 
@@ -156,6 +205,10 @@
             SC[p, t] = val
             G[p, t, l] = val
 
+    def coarse_part(p):
+        j, _ = slot_of(p)
+        CPP[p] = dot(basis[j], SC[p].reshape(rows_here, cols))
+
     def send_own(p):
         src = SC.at[p]
         dst = G.at[p, :, l]
@@ -225,7 +278,7 @@
     def z_wait(buf, k):
         wait_recv(buf.at[: (Z - 1) * X], cr.at[k])
 
-    load_p.wait()
+    loads[3].wait()
 
     for i in range(4):
         for t in range(tiles):
@@ -237,26 +290,67 @@
     to_right = rcopy(SB1, H1.at[:4], hs.at[1], hr.at[1], (right, l))
     to_left.start()
     to_right.start()
+    tell(0)
+    loads[4].wait()
     IF[l] = inv[...]
-    loc_spread(lambda peer: inv, IF, 0)
+    for k, peer in enumerate((lp, lm, sib)):
+        rcopy(inv, IF.at[l], cs.at[0], ir.at[k], (o, peer)).start()
 
     def first(p, carry):
         residual(p, False)
+        return carry
+
+    def first_send(p, carry):
         send_own(p)
         return carry
-
-    lax.fori_loop(0, 4, first, 0)
 
     def second(p, carry):
         residual(p, False)
         return carry
 
-    lax.fori_loop(12, 16, second, 0)
+    def second_part(p, carry):
+        coarse_part(p)
+        return carry
+
+    residual(0, False)
+    send_own(0)
+    lax.fori_loop(1, 4, first, 0)
+    heard(0)
+    tell(1)
+    wait_recv(IF.at[lm], ir.at[0])
+    rcopy(IF.at[lm], IF.at[lm], cs.at[0], ir.at[3], (o, lp)).start()
+    rcopy(IF.at[lm], IF.at[lm], cs.at[0], ir.at[4], (o, sib)).start()
+    lax.fori_loop(1, 4, first_send, 0)
+    wait_recv(IF.at[lp], ir.at[1])
+    rcopy(IF.at[lp], IF.at[lp], cs.at[0], ir.at[5], (o, sib)).start()
+    stack = slots * modes * tiles
+    spread = lax.broadcasted_iota(jnp.int32, (rl, rows_here), 1) % rl
+    spread = (spread == lax.broadcasted_iota(jnp.int32, (rl, rows_here), 0)).astype(F32)
+    loads[5].wait()
+    wide = dot(basis_in[...].reshape(stack, rl), spread)
+    at_row = lax.broadcasted_iota(jnp.int32, (stack, rows_here), 0) % tiles
+    at_lane = lax.broadcasted_iota(jnp.int32, (stack, rows_here), 1) // rl
+    wide = jnp.where(at_row == at_lane, wide, 0.0).reshape(slots * modes, tiles, rows_here)
+    wide = jnp.sum(wide, axis=1)
+    basis[...] = jnp.zeros_like(basis)
+    for j in range(slots):
+        basis[j, :modes] = wide[j * modes : (j + 1) * modes]
+
+    lax.fori_loop(12, 14, second, 0)
+    lax.fori_loop(12, 14, first_send, 0)
+    lax.fori_loop(14, 16, second, 0)
+    heard(1)
+    tell(2)
+    wait_recv(IF.at[l2], ir.at[3])
+    rcopy(IF.at[l2], IF.at[l2], cs.at[0], ir.at[6], (o, sib)).start()
+    lax.fori_loop(0, 4, second_part, 0)
+    lax.fori_loop(12, 16, second_part, 0)
 
     ACC[...] = jnp.zeros_like(ACC)
     IT[...] = jnp.zeros_like(IT)
     W[...] = jnp.zeros_like(W)
-    loc_wait(IF, 0)
+    for k in (2, 4, 5, 6):
+        wait_recv(IF.at[0], ir.at[k])
     for k in range(n_loc):
         IT[k * ic : (k + 1) * ic, :io] = IF[k].T
 
@@ -266,31 +360,22 @@
             W[s, m : m + 1, :] = IT[pl.ds(row, 1), :]
         return carry
 
+    loads[6].wait()
     lax.fori_loop(0, subs, fill, 0)
 
+    heard(2)
     to_left.wait_recv()
     to_right.wait_recv()
 
     def third(p, carry):
         residual(p, True)
-        send_own(p)
+        coarse_part(p)
         return carry
 
     lax.fori_loop(4, 12, third, 0)
 
-    def fourth(p, carry):
-        send_own(p)
-        return carry
-
-    lax.fori_loop(12, 16, fourth, 0)
-
-    def coarse_part(j, carry):
-        vals = SC[pos_of(j)].reshape(rows_here, cols)
-        vals = jnp.where(j < cnt, vals, 0.0)
-        CP[j] = dot(basis[j], vals)
-        return carry
-
-    lax.fori_loop(0, slots, coarse_part, 0)
+    for j in range(slots):
+        CP[j] = jnp.where(j < cnt, CPP[pos_of(jnp.int32(j))], 0.0)
     CT[...] = CP[...].reshape(slots * pad, cols).T.reshape(n_loc, nb, slots * pad)
     R1[l] = CT[l]
     loc_spread(lambda peer: CT.at[peer], R1, 1)
@@ -310,13 +395,17 @@
     def solve():
         z_wait(R2, 3)
 
+        def rows_at(at):
+            return W[pl.ds(jnp.clip(at, 0, subs), slots)].reshape(slots * pad, 128)
+
         def body(k, carry):
             total, at = carry
-            rows = W[pl.ds(jnp.clip(at, 0, subs), slots)].reshape(slots * pad, 128)
-            total = total + dot(R2[k], rows)
-            return total, at + load_of(k)
-
-        total, _ = lax.fori_loop(0, n_sub, body, (jnp.zeros((nb, 128), F32), jnp.int32(0)))
+            later = at + load_of(2 * k)
+            rhs = jnp.concatenate([R2[2 * k], R2[2 * k + 1]], axis=1)
+            rows = jnp.concatenate([rows_at(at), rows_at(later)], axis=0)
+            return total + stacked_dot(rhs, rows), later + load_of(2 * k + 1)
+
+        total, _ = lax.fori_loop(0, n_sub // 2, body, (jnp.zeros((nb, 128), F32), jnp.int32(0)))
         R3[o] = total
         x_spread(R3, 4)
 
@@ -339,24 +428,18 @@
         wanted = jnp.broadcast_to(numbers[:1], (128, 128))
         rows = lax.broadcasted_iota(jnp.int32, (128, 128), 0)
 
+        def hot(k):
+            return ((wanted == rows + k * io) & (rows < io)).astype(F32).astype(BF16)
+
         def body(k, total):
-            hot = ((wanted == rows + k * io) & (rows < io)).astype(F32).astype(jnp.bfloat16)
-            v = R3[k]
-            h = v.astype(jnp.bfloat16)
-            r = v - h.astype(F32)
-            m = r.astype(jnp.bfloat16)
-            q = (r - m.astype(F32)).astype(jnp.bfloat16)
-            for part in (h, m, q):
-                total = total + lax.dot_general(
-                    part, hot, (((1,), (0,)), ((), ())), preferred_element_type=F32
-                )
-            return total
-
-        mv = lax.fori_loop(0, n_sub, body, jnp.zeros((nb, 128), F32))
+            v = jnp.concatenate([R3[2 * k], R3[2 * k + 1]], axis=1)
+            parts = jnp.concatenate(split3(v), axis=0)
+            picked = mul16(parts, jnp.concatenate([hot(2 * k), hot(2 * k + 1)], axis=0))
+            return total + ((picked[2 * nb :] + picked[nb : 2 * nb]) + picked[:nb])
+
+        mv = lax.fori_loop(0, n_sub // 2, body, jnp.zeros((nb, 128), F32))
         M4[l] = mv
         loc_spread(lambda peer: M4.at[l], M4, 6)
-
-    MV_AT = 10
 
     def modes_ready():
         loc_wait(M4, 6)
@@ -366,48 +449,64 @@
             correct(p)
             return carry
 
-        lax.fori_loop(0, MV_AT - 1, body, 0)
+        lax.fori_loop(4, 8, body, 0)
+        rcopy(V.at[4:8], H2.at[4:], hs.at[2], hr.at[2], (left, l)).start()
+        lax.fori_loop(8, MV_AT - LAG + 1, body, 0)
 
     def send_halo():
         for i in range(4):
             p = pos_of(cnt - 4 + i)
             for t in range(tiles):
                 SB2[i, t] = V[p, t]
-        rcopy(V.at[8:12], H2.at[4:], hs.at[2], hr.at[2], (left, l)).start()
         rcopy(SB2, H2.at[:4], hs.at[3], hr.at[3], (right, l)).start()
 
-    chain = {2: reduce_loc, 3: gather_z, 4: solve, 5: gather_z2, 6: select, MV_AT: modes_ready, 13: send_halo}
-
-    load_s.wait()
+    def late(p):
+        def run():
+            correct(p)
+            correct(p + 1)
+
+        return run
+
+    chain = {2: reduce_loc, 3: gather_z, 5: solve, 6: gather_z2, 8: select, MV_AT: modes_ready, 11 + LAG: send_halo}
+    chain.update({12 + LAG: late(0), 13 + LAG: late(2)})
+
+    loads[7].wait()
 
     def step(s, carry):
         @pl.when(s < slots)
         def _():
             forward(s)
 
-        @pl.when((s >= 1) & (s < slots + 1))
+        @pl.when(s < slots - EARLY)
         def _():
-            halves(s - 1)
-
-        @pl.when(s >= 2)
+            send_own(jnp.where(s < 8, s + 4, s + EARLY))
+
+        @pl.when((s >= LAG - 1) & (s < slots + LAG - 1))
         def _():
-            apply_local(s - 2)
+            halves(s - (LAG - 1))
+
+        @pl.when(s >= LAG)
+        def _():
+            apply_local(s - LAG)
 
         @pl.when(s > MV_AT)
         def _():
-            correct(s - 2)
+            correct(s - LAG)
 
         for at, what in chain.items():
             pl.when(s == at)(what)
         return carry
 
-    lax.fori_loop(0, slots + 2, step, 0)
+    lax.fori_loop(0, slots + LAG, step, 0)
 
     IS1[l] = ACC[: rl // 2, :] + ACC[rl // 2 :, :]
     loc_spread(lambda peer: IS1.at[l], IS1, 7)
 
     wait_recv(H2.at[4:], hr.at[2])
     wait_recv(H2.at[:4], hr.at[3])
+
+    def put(k, a, b):
+        return pltpu.make_async_copy(OUT.at[a:b], out.at[a:b], od.at[k])
 
     def finish(j, carry):
         live = j < cnt
@@ -416,10 +515,11 @@
             linked, own, q, hq, mt = link(j, live, t)
             other = jnp.where(own, V[pos_of(q), mt], H2[hq, mt])
             val = V[p, t] + jnp.where(linked, other, 0.0)
-            out[j, t] = jnp.where(live, val, 0.0)
+            OUT[j, t] = jnp.where(live, val, 0.0)
         return carry
 
     lax.fori_loop(0, 6, finish, 0)
+    put(0, 0, 6).start()
     loc_wait(IS1, 7)
     total = IS1[0]
     for i in range(1, n_loc):
@@ -429,6 +529,7 @@
         peer = z * X + (x + i) % X
         rcopy(IS2.at[x], IS2.at[x], cs.at[8], cr.at[8], (peer, l)).start()
     lax.fori_loop(6, 11, finish, 0)
+    put(1, 6, 11).start()
     wait_recv(IS2.at[: X - 1], cr.at[8])
     total = IS2[0]
     for i in range(1, X):
@@ -438,15 +539,19 @@
         peer = ((z + i) % Z) * X + x
         rcopy(IS3.at[z], IS3.at[z], cs.at[9], cr.at[9], (peer, l)).start()
     lax.fori_loop(11, 16, finish, 0)
+    put(2, 11, 16).start()
     wait_recv(IS3.at[: Z - 1], cr.at[9])
     total = IS3[0]
     for i in range(1, Z):
         total = total + IS3[i]
     inner_out[...] = jnp.sum(total, axis=0, keepdims=True)
 
+    put(0, 0, 6).wait()
+    put(1, 6, 11).wait()
+    put(2, 11, 16).wait()
     wait_send(PV.at[:4], hs.at[0])
     wait_send(SB1, hs.at[1])
-    wait_send(V.at[8:12], hs.at[2])
+    wait_send(V.at[4:8], hs.at[2])
     wait_send(SB2, hs.at[3])
     wait_send(G.at[:, :, : n_loc - 1], ysend)
     wait_send(IF.at[: n_loc - 1], cs.at[0])
@@ -468,11 +573,10 @@
     io, ic = coarse_inverse.shape
     nb = cols // n_loc
     Z = n_sub // X
-    basis = jnp.pad(rigid_basis, ((0, 0), (0, 8 - modes), (0, 0), (0, 0))).reshape(slots, 8, tiles * rl)
     vmem = lambda *shape: pltpu.VMEM(shape, F32)
     dma = lambda *shape: pltpu.SemaphoreType.DMA(shape)
     in_v = pl.BlockSpec(memory_space=pltpu.VMEM)
-    in_s = pl.BlockSpec(memory_space=pltpu.SMEM)
+    hbm = pl.BlockSpec(memory_space=pltpu.HBM)
     any_ = pl.BlockSpec(memory_space=pl.ANY)
     precond, inner = pl.pallas_call(
         functools.partial(kernel, n_sub, n_loc),
@@ -480,9 +584,17 @@
             jax.ShapeDtypeStruct(partials.shape, F32),
             jax.ShapeDtypeStruct((1, cols), F32),
         ),
-        in_specs=[any_, any_, in_v, in_v, in_s, in_s, in_s, in_s],
-        out_specs=(in_v, in_v),
+        in_specs=[hbm] * 8,
+        out_specs=(any_, in_v),
         scratch_shapes=[
+            vmem(*rigid_basis.shape),
+            vmem(io, ic),
+            pltpu.SMEM(placement.shape, jnp.int32),
+            pltpu.SMEM(nsub.shape[::-1], jnp.int32),
+            pltpu.SMEM(ntile.shape[::-1], jnp.int32),
+            pltpu.SMEM(cnum.shape, jnp.int32),
+            vmem(slots, 8, tiles * rl),
+            vmem(slots, tiles, rl, cols),
             vmem(slots, tiles, rl, cols),
             vmem(slots, tiles, rl, tiles * n_loc * rl),
             vmem(slots, tiles, rl, cols),
@@ -492,6 +604,7 @@
             vmem(8, tiles, rl, cols),
             vmem(4, tiles, rl, cols),
             vmem(4, tiles, rl, cols),
+            vmem(slots, 8, cols),
             vmem(slots, 8, cols),
             vmem(n_loc, nb, slots * 8),
             vmem(n_loc, nb, slots * 8),
@@ -506,7 +619,10 @@
             vmem(X, rl // 2, cols),
             vmem(Z, rl // 2, cols),
             vmem(rl, cols),
-            dma(2),
+            dma(8),
+            pltpu.SemaphoreType.REGULAR((3,)),
+            dma(3),
+            dma(7),
             dma(4),
             dma(4),
             dma(10),
@@ -521,7 +637,7 @@
         compiler_params=pltpu.CompilerParams(
             collective_id=0, has_side_effects=True, vmem_limit_bytes=56 * 1024 * 1024
         ),
-    )(partials, local_schur, basis, coarse_inverse, placement, nsub.T, ntile.T, cnum)
+    )(partials, local_schur, rigid_basis, coarse_inverse, placement, nsub.T, ntile.T, cnum)
     return precond, inner.reshape(cols)
 
 

time: 162 us -> 113 us (0.70)
  Pallas kernels: 156 us -> 109 us
  local copies, waits for them, and re-layouts: 5.58 us -> 3.71 us
    pallas_call x1, Pallas kernels: 156 us -> 109 us  [local(): pl.pallas_call(functools.partial(kernel, n_sub, n_loc), out_shape=(jax.Sh...]
where the time goes in v2:
time: 113 us
  Pallas kernels  109 us (96%)
  local copies, waits for them, and re-layouts  3.71 us (3%)
    pallas_call x1, Pallas kernels, local(): pl.pallas_call(functools.partial(kernel, n_sub, n_loc), out_shape=(jax.Sh...  109 us
    unnamed x4, local copies, waits for them, and re-layouts  3.71 us

profile of v2, /device:TPU:8, one launch (start us, length us, event | category | flops | bytes accessed | tf_op | source)
XLA Modules:
  0.0 113.3 jit_solution(4895186796087360618)
XLA Ops:
  0.6 109.0 %shard_map.95 = (f32[16,8,16,256]{3,2,1,0:T(8,128)}, f32[1,256]{1,0:T(1,128)}) custom-call(f32[16,8,16,256]{3,2,1,0:T(8,128)} %part_hbm.1, f32[16,8,16,1024]{3,2,1,0:T(8,128)} %schur_hbm.1, f32[16,6,8,16]{3,2,1,0:T(8,128)} %basis_hbm.1, f32[48,192]{1,0:T(8,128)} %inv_hbm.1, s32[32]{0:T(128)} %placement_hbm.1, s32[8,256]{1,0:T(8,128)} %bitcast.3, ...), custom_call_target="tpu_custom_call" | custom-call | tf_op jit(solution)/shard_map/pallas_call | solution.py:581
  109.6 0.0 copy-start
  109.6 3.1 %copy.12 = f32[16,8,16,256]{3,2,1,0:T(8,128)} copy(f32[16,8,16,256]{3,2,1,0:T(8,128)} %get-tuple-element.8) | data formatting | bytes 4194304
  112.8 0.0 copy-done
  112.8 0.6 copy.13
Async XLA Ops:
  109.6 3.2 %copy-start = (f32[1,256]{1,0:T(1,128)S(1)}, f32[1,256]{1,0:T(1,128)}, u32[]{:S(2)}) copy-start(f32[1,256]{1,0:T(1,128)} %get-tuple-element.5) | copy-start | bytes 3076

commit v3 on v2

--- a/solution.py
+++ b/solution.py
@@ -7,9 +7,10 @@
 from jax.sharding import PartitionSpec as P
 
 SLAB = 4
-EARLY = 6
+EARLY = 5
 LAG = 4
-MV_AT = 12
+MV_AT = 13
+CUTS = ((0, 6), (6, 12), (12, 16))
 X = 4
 MESH = pl.DeviceIdType.MESH
 HI = lax.Precision.HIGHEST
@@ -336,9 +337,9 @@
     for j in range(slots):
         basis[j, :modes] = wide[j * modes : (j + 1) * modes]
 
-    lax.fori_loop(12, 14, second, 0)
-    lax.fori_loop(12, 14, first_send, 0)
-    lax.fori_loop(14, 16, second, 0)
+    lax.fori_loop(12, 13, second, 0)
+    lax.fori_loop(12, 13, first_send, 0)
+    lax.fori_loop(13, 16, second, 0)
     heard(1)
     tell(2)
     wait_recv(IF.at[l2], ir.at[3])
@@ -467,7 +468,7 @@
 
         return run
 
-    chain = {2: reduce_loc, 3: gather_z, 5: solve, 6: gather_z2, 8: select, MV_AT: modes_ready, 11 + LAG: send_halo}
+    chain = {3: reduce_loc, 4: gather_z, 6: solve, 7: gather_z2, 9: select, MV_AT: modes_ready, 11 + LAG: send_halo}
     chain.update({12 + LAG: late(0), 13 + LAG: late(2)})
 
     loads[7].wait()
@@ -502,8 +503,6 @@
     IS1[l] = ACC[: rl // 2, :] + ACC[rl // 2 :, :]
     loc_spread(lambda peer: IS1.at[l], IS1, 7)
 
-    wait_recv(H2.at[4:], hr.at[2])
-    wait_recv(H2.at[:4], hr.at[3])
 
     def put(k, a, b):
         return pltpu.make_async_copy(OUT.at[a:b], out.at[a:b], od.at[k])
@@ -518,8 +517,6 @@
             OUT[j, t] = jnp.where(live, val, 0.0)
         return carry
 
-    lax.fori_loop(0, 6, finish, 0)
-    put(0, 0, 6).start()
     loc_wait(IS1, 7)
     total = IS1[0]
     for i in range(1, n_loc):
@@ -528,8 +525,6 @@
     for i in range(1, X):
         peer = z * X + (x + i) % X
         rcopy(IS2.at[x], IS2.at[x], cs.at[8], cr.at[8], (peer, l)).start()
-    lax.fori_loop(6, 11, finish, 0)
-    put(1, 6, 11).start()
     wait_recv(IS2.at[: X - 1], cr.at[8])
     total = IS2[0]
     for i in range(1, X):
@@ -538,17 +533,19 @@
     for i in range(1, Z):
         peer = ((z + i) % Z) * X + x
         rcopy(IS3.at[z], IS3.at[z], cs.at[9], cr.at[9], (peer, l)).start()
-    lax.fori_loop(11, 16, finish, 0)
-    put(2, 11, 16).start()
+    wait_recv(H2.at[4:], hr.at[2])
+    wait_recv(H2.at[:4], hr.at[3])
+    for k, (a, b) in enumerate(CUTS):
+        lax.fori_loop(a, b, finish, 0)
+        put(k, a, b).start()
     wait_recv(IS3.at[: Z - 1], cr.at[9])
     total = IS3[0]
     for i in range(1, Z):
         total = total + IS3[i]
     inner_out[...] = jnp.sum(total, axis=0, keepdims=True)
 
-    put(0, 0, 6).wait()
-    put(1, 6, 11).wait()
-    put(2, 11, 16).wait()
+    for k, (a, b) in enumerate(CUTS):
+        put(k, a, b).wait()
     wait_send(PV.at[:4], hs.at[0])
     wait_send(SB1, hs.at[1])
     wait_send(V.at[4:8], hs.at[2])

time: 113 us -> 108 us (0.956); the launches traced: 113 us -> 106 us
  Pallas kernels: 109 us -> 102 us
    pallas_call x1, Pallas kernels: 109 us -> 102 us  [local(): pl.pallas_call(functools.partial(kernel, n_sub, n_loc), out_shape=(jax.Sh...]
where the time goes in v3:
time: 108 us; the launch traced here: 106 us
  Pallas kernels  102 us (94%)
  local copies, waits for them, and re-layouts  3.71 us (3%)
    pallas_call x1, Pallas kernels, local(): pl.pallas_call(functools.partial(kernel, n_sub, n_loc), out_shape=(jax.Sh...  102 us
    unnamed x4, local copies, waits for them, and re-layouts  3.71 us

profile of v3, /device:TPU:8, one launch (start us, length us, event | category | flops | bytes accessed | tf_op | source)
XLA Modules:
  0.0 106.2 jit_solution(7178626803590766000)
XLA Ops:
  0.6 101.8 %shard_map.95 = (f32[16,8,16,256]{3,2,1,0:T(8,128)}, f32[1,256]{1,0:T(1,128)}) custom-call(f32[16,8,16,256]{3,2,1,0:T(8,128)} %part_hbm.1, f32[16,8,16,1024]{3,2,1,0:T(8,128)} %schur_hbm.1, f32[16,6,8,16]{3,2,1,0:T(8,128)} %basis_hbm.1, f32[48,192]{1,0:T(8,128)} %inv_hbm.1, s32[32]{0:T(128)} %placement_hbm.1, s32[8,256]{1,0:T(8,128)} %bitcast.3, ...), custom_call_target="tpu_custom_call" | custom-call | tf_op jit(solution)/shard_map/pallas_call | solution.py:578
  102.4 0.0 copy-start
  102.5 3.1 %copy.12 = f32[16,8,16,256]{3,2,1,0:T(8,128)} copy(f32[16,8,16,256]{3,2,1,0:T(8,128)} %get-tuple-element.8) | data formatting | bytes 4194304
  105.6 0.0 copy-done
  105.6 0.6 copy.13
Async XLA Ops:
  102.4 3.2 %copy-start = (f32[1,256]{1,0:T(1,128)S(1)}, f32[1,256]{1,0:T(1,128)}, u32[]{:S(2)}) copy-start(f32[1,256]{1,0:T(1,128)} %get-tuple-element.5) | copy-start | bytes 3076

commit v4 on v3

--- a/solution.py
+++ b/solution.py
@@ -500,7 +500,7 @@
 
     lax.fori_loop(0, slots + LAG, step, 0)
 
-    IS1[l] = ACC[: rl // 2, :] + ACC[rl // 2 :, :]
+    IS1[l] = jnp.sum(ACC[...], axis=0, keepdims=True)
     loc_spread(lambda peer: IS1.at[l], IS1, 7)
 
 
@@ -542,7 +542,7 @@
     total = IS3[0]
     for i in range(1, Z):
         total = total + IS3[i]
-    inner_out[...] = jnp.sum(total, axis=0, keepdims=True)
+    inner_out[...] = total
 
     for k, (a, b) in enumerate(CUTS):
         put(k, a, b).wait()
@@ -612,9 +612,9 @@
             vmem(n_loc, io, ic),
             vmem(n_loc * ic, 128),
             vmem(subs + slots, 8, 128),
-            vmem(n_loc, rl // 2, cols),
-            vmem(X, rl // 2, cols),
-            vmem(Z, rl // 2, cols),
+            vmem(n_loc, 1, cols),
+            vmem(X, 1, cols),
+            vmem(Z, 1, cols),
             vmem(rl, cols),
             dma(8),
             pltpu.SemaphoreType.REGULAR((3,)),

time: 108 us -> 106 us (0.981)
  Pallas kernels: 102 us -> 99.9 us
    pallas_call x1, Pallas kernels: 102 us -> 99.9 us  [local(): pl.pallas_call(functools.partial(kernel, n_sub, n_loc), out_shape=(jax.Sh...]
where the time goes in v4:
time: 106 us; the launch traced here: 104 us
  Pallas kernels  99.9 us (94%)
  local copies, waits for them, and re-layouts  3.71 us (4%)
    pallas_call x1, Pallas kernels, local(): pl.pallas_call(functools.partial(kernel, n_sub, n_loc), out_shape=(jax.Sh...  99.9 us
    unnamed x4, local copies, waits for them, and re-layouts  3.71 us

profile of v4, /device:TPU:8, one launch (start us, length us, event | category | flops | bytes accessed | tf_op | source)
XLA Modules:
  0.0 104.3 jit_solution(1101291325149823774)
XLA Ops:
  0.6 99.9 %shard_map.95 = (f32[16,8,16,256]{3,2,1,0:T(8,128)}, f32[1,256]{1,0:T(1,128)}) custom-call(f32[16,8,16,256]{3,2,1,0:T(8,128)} %part_hbm.1, f32[16,8,16,1024]{3,2,1,0:T(8,128)} %schur_hbm.1, f32[16,6,8,16]{3,2,1,0:T(8,128)} %basis_hbm.1, f32[48,192]{1,0:T(8,128)} %inv_hbm.1, s32[32]{0:T(128)} %placement_hbm.1, s32[8,256]{1,0:T(8,128)} %bitcast.3, ...), custom_call_target="tpu_custom_call" | custom-call | tf_op jit(solution)/shard_map/pallas_call | solution.py:578
  100.6 0.0 copy-start
  100.6 3.1 %copy.12 = f32[16,8,16,256]{3,2,1,0:T(8,128)} copy(f32[16,8,16,256]{3,2,1,0:T(8,128)} %get-tuple-element.8) | data formatting | bytes 4194304
  103.7 0.0 copy-done
  103.7 0.6 copy.13
Async XLA Ops:
  100.6 3.2 %copy-start = (f32[1,256]{1,0:T(1,128)S(1)}, f32[1,256]{1,0:T(1,128)}, u32[]{:S(2)}) copy-start(f32[1,256]{1,0:T(1,128)} %get-tuple-element.5) | copy-start | bytes 3076
